TPU v7x, 32 devices: a whole 2x2x4 slice. The times are simulated.
32 devices in a mesh: req: 8 (over y, x, core), head: 4 (over z).
Axes of the slice: x: 2, y: 2, z: 4, core: 2. Of those that a mesh axis runs over, the one named last changes fastest.
Arguments:
- queries: bfloat16 [1024, 16384], P(('req', 'head')), may hold values from -15 to 15
- cache_keys: bfloat16 [8, 32768, 1024], P(None, 'req', 'head'), may hold values from -6 to 6
- cache_values: bfloat16 [8, 32768, 1024], P(None, 'req', 'head'), may hold values from -6 to 6
- tree_keys: bfloat16 [1024, 1024], P('req', 'head'), may hold values from -10 to 10
- tree_values: bfloat16 [1024, 1024], P('req', 'head'), may hold values from -6 to 6
- parents: int32 [8, 128], replicated, may hold values from -1 to 126, as said below
- tree_sizes: int32 [8], replicated, may hold values from 16 to 128
- cache_lens: int32 [8], replicated, may hold values from 2 to 32768
Outputs:
- attended: bfloat16 [1024, 16384], P('req', 'head')
Inputs may be any that keep to these rules, and one draw needn't show every extreme that they name: parents[a, 0] = -1 (the root); for node i >= 1, parents[a, i] is a node of 0 to i - 1.
All inputs are finite; a program needn't handle non-finite values.
Results may differ from a plain program's by a relative error of at most 0.003.
Values may be sent and summed in bfloat16 or wider, within the bound.
No kernel may reach another device: no remote copies, remote signals or barrier semaphores. Data moves between devices by JAX's collectives and lax.ppermute only.
A program may use at most 192 MiB of HBM per device.

v0:
```python
import functools
import math

import jax
import jax.numpy as jnp
from jax import lax
from jax.experimental import pallas as pl
from jax.experimental.pallas import tpu as pltpu
from jax.sharding import PartitionSpec as P

NH = 128
KVH = 8
HD = 128
GROUP = NH // KVH
WIDE = GROUP * HD
LANES = 128
NODES = 32
ROWS = GROUP * NODES

negative_fill = -1e30
softmax_scale = 1.0 / math.sqrt(HD)
exp2_scale = softmax_scale * math.log2(math.e)
wire = jnp.bfloat16


def lane_max(scores):
    best = scores[:, :LANES]
    for at in range(LANES, scores.shape[1], LANES):
        best = jnp.maximum(best, scores[:, at : at + LANES])
    return best


def place_logs(logs):
    lane = lax.broadcasted_iota(jnp.int32, logs[0].shape, 1) % GROUP
    placed = logs[0]
    for head in range(1, GROUP):
        placed = jnp.where(lane == head, logs[head], placed)
    return placed


def split_logs(logs):
    high = logs.astype(wire).astype(jnp.float32)
    rest = logs - high
    middle = rest.astype(wire).astype(jnp.float32)
    group = lax.broadcasted_iota(jnp.int32, logs.shape, 1) // GROUP
    parts = jnp.where(group == 0, high, jnp.where(group == 1, middle, rest - middle))
    return parts.astype(wire)


def join_logs(parts):
    parts = parts.astype(jnp.float32)
    return parts + pltpu.roll(parts, LANES - GROUP, 1) + pltpu.roll(parts, LANES - 2 * GROUP, 1)


def unit_kernel(listed, merging, chunk, ids_ref, lens_ref, sizes_ref, base_ref, *refs):
    q_refs, refs = refs[:listed], refs[listed:]
    k_ref, v_ref, refs = refs[0], refs[1], refs[2:]
    r_ref, refs = (refs[0], refs[1:]) if merging else (None, refs)
    o_ref, q_ref, p_ref, x_ref, a_ref, f_ref, t_ref, h_ref, g_ref, m_ref = refs
    unit = pl.program_id(0)
    request = ids_ref[unit]
    block = k_ref.shape[1]
    node_count = q_ref.shape[0]
    live = jnp.clip(lens_ref[request] - base_ref[0], 0, block)
    tiles = (sizes_ref[request] + NODES - 1) // NODES
    step = 256
    part = min(block, 512)
    part_chunks = (live + part - 1) // part
    whole_chunks = live // chunk

    def score(queries, at, width):
        return lax.dot_general(
            queries,
            k_ref[0, pl.ds(at, width), :],
            (((1,), (1,)), ((), ())),
            preferred_element_type=jnp.float32,
        )

    def weigh(scores):
        return [
            jnp.exp2(scores[:, i : i + LANES] * exp2_scale - h_ref[...]).astype(jnp.bfloat16)
            for i in range(0, scores.shape[1], LANES)
        ]

    def masked(scores, at):
        column = lax.broadcasted_iota(jnp.int32, scores.shape, 1)
        return jnp.where(column < live - at, scores, negative_fill)

    def shift_of(best):
        peaks = jnp.max(best, axis=1, keepdims=True) * exp2_scale
        return jnp.broadcast_to(peaks, best.shape)

    def take(t):
        start = pl.multiple_of(t * NODES, NODES)
        return jnp.concatenate(
            [q_ref[pl.ds(start, NODES), h * HD : (h + 1) * HD] for h in range(GROUP)], axis=0
        )

    def sample(t):
        queries = take(t)
        return queries, shift_of(masked(score(queries, 0, LANES), 0))

    def chunk_sums(at, place):
        for i in range(0, chunk, step):
            for j, piece in enumerate(weigh(score(t_ref[...], at + i, step))):
                p_ref[:, place + i + j * LANES : place + i + (j + 1) * LANES] = piece
        return jnp.dot(
            p_ref[:, place : place + chunk], x_ref[pl.ds(at, chunk), :], preferred_element_type=jnp.float32
        )

    def whole_block():
        chunks = block // chunk
        for c in range(chunks):
            sums = chunk_sums(c * chunk, c * chunk)
            if c > 0:
                sums = a_ref[...] + sums
            if c < chunks - 1:
                a_ref[...] = sums
            else:
                f_ref[...] = sums

    def part_block():
        f_ref[...] = jnp.zeros(f_ref.shape, jnp.float32)

        @pl.loop(0, whole_chunks)
        def _(c):
            f_ref[...] += chunk_sums(pl.multiple_of(c * chunk, chunk), 0)

        @pl.loop(whole_chunks * (chunk // part), part_chunks)
        def _(c):
            at = pl.multiple_of(c * part, part)
            weights = jnp.concatenate(weigh(masked(score(t_ref[...], at, part), at)), axis=1)
            f_ref[...] += jnp.dot(weights, x_ref[pl.ds(at, part), :], preferred_element_type=jnp.float32)

    def exact_shift():
        g_ref[...] = jnp.full(g_ref.shape, negative_fill, jnp.float32)

        @pl.loop(0, part_chunks)
        def _(c):
            at = pl.multiple_of(c * part, part)
            best = lane_max(masked(score(t_ref[...], at, part), at))
            g_ref[...] = jnp.maximum(g_ref[...], best)

        h_ref[...] = shift_of(g_ref[...])

    def finish(t):
        rows = pl.ds(pl.multiple_of(jnp.maximum(t, 0) * NODES, NODES), NODES)
        totals = f_ref[:, LANES:]
        m_ref[...] = jnp.maximum(m_ref[...], jnp.where(t >= 0, totals, 0.0))
        inverse = 1.0 / totals
        logs = g_ref[...] * math.log(2.0) + jnp.log(totals)
        other_logs = join_logs(r_ref[0, rows, WIDE:]) if merging else None
        head_logs = []
        for h in range(GROUP):
            at = slice(h * NODES, (h + 1) * NODES)
            columns = slice(h * HD, (h + 1) * HD)
            partial = f_ref[at, :LANES] * inverse[at]
            log = logs[at]
            if merging:
                other = jnp.broadcast_to(other_logs[:, h : h + 1], (NODES, LANES))
                top = jnp.maximum(log, other)
                own_weight = jnp.exp(log - top)
                other_weight = jnp.exp(other - top)
                total = own_weight + other_weight
                mixed = partial * own_weight + r_ref[0, rows, columns].astype(jnp.float32) * other_weight
                partial = mixed / total
                log = top + jnp.log(total)
            o_ref[0, rows, columns] = partial.astype(wire)
            head_logs.append(log)
        o_ref[0, rows, WIDE:] = split_logs(place_logs(head_logs))

    @pl.when(unit == 0)
    def _():
        x_ref[:, HD:] = jnp.ones((block, LANES), x_ref.dtype)

    @pl.when(live == 0)
    def _():
        if merging:
            o_ref[...] = r_ref[...]
        else:
            o_ref[0, :, :WIDE] = jnp.zeros((node_count, WIDE), wire)
            o_ref[0, :, WIDE:] = split_logs(jnp.full((node_count, LANES), negative_fill, jnp.float32))

    @pl.when(live > 0)
    def _():
        if listed == 1:
            q_ref[...] = q_refs[0][...]
        else:
            for i in range(listed):

                @pl.when(unit == i)
                def _():
                    q_ref[...] = q_refs[i][...]

        x_ref[:, :HD] = v_ref[0]
        m_ref[...] = jnp.zeros(m_ref.shape, jnp.float32)

    @pl.when(live == block)
    def _():
        queries, shift = sample(0)
        t_ref[...] = queries
        h_ref[...] = shift

        @pl.loop(0, tiles)
        def _(t):
            finish(t - 1)
            g_ref[...] = h_ref[...]
            queries, shift = sample(jnp.minimum(t + 1, tiles - 1))
            whole_block()
            t_ref[...] = queries
            h_ref[...] = shift

        finish(tiles - 1)

    @pl.loop(0, 2)
    def _(exact):
        overflowed = jnp.logical_not(jnp.max(m_ref[...]) < 2.0**100)
        first = jnp.logical_and(exact == 0, live < block)
        again = jnp.logical_and(exact == 1, overflowed)

        @pl.when(jnp.logical_and(live > 0, jnp.logical_or(first, again)))
        def _():
            @pl.loop(0, tiles)
            def _(t):
                t_ref[...] = take(t)

                @pl.when(exact == 0)
                def _():
                    h_ref[...] = shift_of(masked(score(t_ref[...], 0, LANES), 0))

                @pl.when(exact == 1)
                def _():
                    exact_shift()

                part_block()
                g_ref[...] = h_ref[...]
                finish(t)


def unit_attention(queries, ids, kv_head, cache_keys, cache_values, lens, sizes, base, node_count, received=None):
    units = ids.shape[0] // 2
    block = cache_keys.shape[1]
    chunk = min(block, 1024)
    merging = received is not None
    width = WIDE + LANES

    def cache_map(u, ids_ref, *_):
        return (ids_ref[u], 0, kv_head)

    def unit_map(u, *_):
        return (u, 0, 0)

    def received_map(u, ids_ref, *_):
        return (ids_ref[2 * units] + u, 0, 0)

    if isinstance(queries, list):
        in_specs = [
            pl.BlockSpec((node_count, WIDE), functools.partial(lambda i, u, ids_ref, *_: (ids_ref[units + i], 0), i))
            for i in range(units)
        ]
    else:
        queries = [queries]
        in_specs = [pl.BlockSpec((node_count, WIDE), lambda u, ids_ref, *_: (ids_ref[units + u], 0))]
    operands = queries + [cache_keys, cache_values]
    in_specs = in_specs + [pl.BlockSpec((1, block, HD), cache_map)] * 2
    if merging:
        in_specs.append(pl.BlockSpec((1, node_count, width), received_map))
        operands.append(received)
    grid_spec = pltpu.PrefetchScalarGridSpec(
        num_scalar_prefetch=4,
        grid=(units,),
        in_specs=in_specs,
        out_specs=pl.BlockSpec((1, node_count, width), unit_map),
        scratch_shapes=[
            pltpu.VMEM((node_count, WIDE), jnp.bfloat16),
            pltpu.VMEM((ROWS, block), jnp.bfloat16),
            pltpu.VMEM((block, 2 * LANES), jnp.bfloat16),
            pltpu.VMEM((ROWS, 2 * LANES), jnp.float32),
            pltpu.VMEM((ROWS, 2 * LANES), jnp.float32),
            pltpu.VMEM((ROWS, HD), jnp.bfloat16),
            pltpu.VMEM((ROWS, LANES), jnp.float32),
            pltpu.VMEM((ROWS, LANES), jnp.float32),
            pltpu.VMEM((ROWS, LANES), jnp.float32),
        ],
    )
    return pl.pallas_call(
        functools.partial(unit_kernel, len(queries), merging, chunk),
        grid_spec=grid_spec,
        out_shape=jax.ShapeDtypeStruct((units, node_count, width), wire),
        compiler_params=pltpu.CompilerParams(vmem_limit_bytes=60 * 1024 * 1024),
        cost_estimate=pl.CostEstimate(
            flops=4 * units * node_count * GROUP * block * HD,
            bytes_accessed=units * (4 * block * HD + 4 * node_count * width),
            transcendentals=units * node_count * GROUP * block,
        ),
    )(ids, lens, sizes, base, *operands)


def tree_kernel(first_ref, *refs):
    kv_local = len(refs) - 6
    q_refs = refs[:kv_local]
    k_ref, v_ref, parents_ref, o_ref, l_ref, r_ref = refs[kv_local:]
    rows_owned = q_refs[0].shape[0]
    node_count = k_ref.shape[0]
    steps = (node_count - 1).bit_length()
    node = lax.broadcasted_iota(jnp.int32, (node_count, node_count), 0)
    other = lax.broadcasted_iota(jnp.int32, (node_count, node_count), 1)
    linked = jnp.logical_or(parents_ref[...] == node, node == other)
    reached = linked.astype(jnp.float32)
    for _ in range(steps):
        half = reached.astype(jnp.bfloat16)
        reached = jnp.minimum(jnp.dot(half, half, preferred_element_type=jnp.float32), 1.0)
    r_ref[...] = reached.T
    tile = min(rows_owned, NODES)
    for g in range(kv_local):
        keys = k_ref[:, g * HD : (g + 1) * HD]
        values = v_ref[:, g * HD : (g + 1) * HD]

        @pl.loop(0, jnp.clip((first_ref[1] - first_ref[0] + tile - 1) // tile, 0, rows_owned // tile))
        def _(t):
            start = pl.multiple_of(t * tile, tile)
            first = pl.multiple_of(first_ref[0] + start, tile)
            queries = jnp.concatenate(
                [q_refs[g][pl.ds(start, tile), h * HD : (h + 1) * HD] for h in range(GROUP)], axis=0
            )
            live = jnp.concatenate([r_ref[pl.ds(first, tile), :]] * GROUP, axis=0) > 0.5
            scores = lax.dot_general(
                queries, keys, (((1,), (1,)), ((), ())), preferred_element_type=jnp.float32
            )
            scores = jnp.where(live, scores, negative_fill)
            peaks = jnp.max(scores, axis=1, keepdims=True)
            weights = jnp.where(live, jnp.exp2((scores - peaks) * exp2_scale), 0.0)
            totals = jnp.maximum(jnp.sum(weights, axis=1, keepdims=True), 1.0)
            sums = jnp.dot(weights.astype(jnp.bfloat16), values, preferred_element_type=jnp.float32)
            partials = sums / totals
            for h in range(GROUP):
                o_ref[g, pl.ds(start, tile), h * HD : (h + 1) * HD] = partials[h * tile : (h + 1) * tile, :]
            logs = jnp.broadcast_to(peaks * softmax_scale + jnp.log(totals), (GROUP * tile, LANES))
            l_ref[g, pl.ds(start, tile), :] = place_logs([logs[h * tile : (h + 1) * tile] for h in range(GROUP)])


def tree_attention(queries, keys, values, parents, first):
    rows = queries[0].shape[0]
    node_count = keys.shape[0]
    kv_local = len(queries)
    vmem = pl.BlockSpec(memory_space=pltpu.VMEM)
    return pl.pallas_call(
        tree_kernel,
        in_specs=[pl.BlockSpec(memory_space=pltpu.SMEM)] + [vmem] * (kv_local + 3),
        out_specs=[vmem, vmem],
        out_shape=[
            jax.ShapeDtypeStruct((kv_local, rows, WIDE), jnp.float32),
            jax.ShapeDtypeStruct((kv_local, rows, LANES), jnp.float32),
        ],
        scratch_shapes=[pltpu.VMEM((node_count, node_count), jnp.float32)],
        compiler_params=pltpu.CompilerParams(vmem_limit_bytes=60 * 1024 * 1024),
        cost_estimate=pl.CostEstimate(flops=10**9, bytes_accessed=10**7, transcendentals=10**6),
    )(first, *queries, keys, values, parents)


def merge_kernel(parts, alive_ref, *refs):
    kv_local = len(parts)
    o_ref = refs[-1]
    tree_ref, tree_logs_ref = refs[-3], refs[-2]
    rows = o_ref.shape[0]
    lane = lax.broadcasted_iota(jnp.int32, (LANES, WIDE), 0)
    head = lax.broadcasted_iota(jnp.int32, (LANES, WIDE), 1) // HD
    spread = jnp.logical_and(lane % GROUP == head, lane < 3 * GROUP).astype(jnp.bfloat16)
    group = lax.broadcasted_iota(jnp.int32, (rows, LANES), 1) // GROUP
    at_part = 0
    for g in range(kv_local):
        part_refs = refs[at_part : at_part + parts[g]]
        at_part += parts[g]
        logs = [join_logs(ref[0, :, WIDE:]) for ref in part_refs] + [tree_logs_ref[g]]
        top = functools.reduce(jnp.maximum, logs)
        weights = [jnp.exp(log - top) for log in logs]
        scale = 1.0 / functools.reduce(jnp.add, weights)
        total = None
        for j, weight in enumerate(weights):
            share = jnp.where(group == 0, weight * scale, 0.0)
            share = share + pltpu.roll(share, GROUP, 1) + pltpu.roll(share, 2 * GROUP, 1)
            wide = jnp.dot(split_logs(share), spread, preferred_element_type=jnp.float32)
            piece = tree_ref[g] if j == parts[g] else part_refs[j][0, :, :WIDE].astype(jnp.float32)
            total = wide * piece if total is None else total + wide * piece
        alive = alive_ref[:, :1] > 0.5
        o_ref[:, g * WIDE : (g + 1) * WIDE] = jnp.where(alive, total, 0.0).astype(o_ref.dtype)


def merge(parts, tree_partials, tree_logs, alive):
    kv_local, rows, _ = tree_partials.shape
    tile = min(rows, NODES)
    flat = [pair for of_head in parts for pair in of_head]
    return pl.pallas_call(
        functools.partial(merge_kernel, [len(of_head) for of_head in parts]),
        grid=(rows // tile,),
        in_specs=[pl.BlockSpec((tile, LANES), lambda i: (i, 0))]
        + [
            pl.BlockSpec((1, tile, WIDE + LANES), functools.partial(lambda u, i: (u, i, 0), unit))
            for _, unit in flat
        ]
        + [
            pl.BlockSpec((kv_local, tile, WIDE), lambda i: (0, i, 0)),
            pl.BlockSpec((kv_local, tile, LANES), lambda i: (0, i, 0)),
        ],
        out_specs=pl.BlockSpec((tile, kv_local * WIDE), lambda i: (i, 0)),
        out_shape=jax.ShapeDtypeStruct((rows, kv_local * WIDE), jnp.bfloat16),
        compiler_params=pltpu.CompilerParams(vmem_limit_bytes=40 * 1024 * 1024),
    )(alive, *[array for array, _ in flat], tree_partials, tree_logs)


def exchange(array, distance):
    owners = lax.axis_size("req")
    return lax.ppermute(array, "req", [(r, r ^ distance) for r in range(owners)])


def body(
    queries, cache_keys, cache_values, tree_keys, tree_values, parents, tree_sizes, cache_lens
):
    owner_index = lax.axis_index("req")
    owners = lax.axis_size("req")
    requests = cache_keys.shape[0]
    block = cache_keys.shape[1]
    kv_local = cache_keys.shape[2] // HD
    node_count = parents.shape[1]
    rows_owned = tree_keys.shape[0]
    head_devices = lax.axis_size("head")
    own = []
    for g in range(kv_local):
        columns = [
            queries[:, (d * kv_local + g) * WIDE : (d * kv_local + g + 1) * WIDE] for d in range(head_devices)
        ]
        mine = jnp.concatenate(columns, axis=1) if kv_local > 1 else queries
        own.append(lax.all_to_all(mine, "head", split_axis=1, concat_axis=0, tiled=True))

    first_row = owner_index * rows_owned
    request = first_row // node_count
    first_node = first_row % node_count
    if rows_owned < node_count:
        every_key = lax.all_gather(tree_keys, "req", axis=0, tiled=True)
        every_value = lax.all_gather(tree_values, "req", axis=0, tiled=True)
        own_keys = lax.dynamic_slice_in_dim(every_key, request * node_count, node_count, 0)
        own_values = lax.dynamic_slice_in_dim(every_value, request * node_count, node_count, 0)
    else:
        own_keys, own_values = tree_keys, tree_values
    size = lax.dynamic_index_in_dim(tree_sizes, request, 0, keepdims=False)
    own_parents = lax.dynamic_slice_in_dim(parents, request, 1, 0)

    def attend_tree(after=None):
        first = jnp.stack([first_node, size])
        if after is not None:
            first, _ = lax.optimization_barrier((first, after))
        return tree_attention(own, own_keys, own_values, own_parents, first)

    alive = first_node + jnp.arange(rows_owned, dtype=jnp.int32) < size
    alive = jnp.broadcast_to(alive[:, None].astype(jnp.float32), (rows_owned, LANES))
    base = (owner_index * block)[None]

    def attend(queries, targets, blocks, kv_head, received=None, offset=0, after=None):
        ids = jnp.stack([jnp.asarray(i, jnp.int32) for i in [*targets, *blocks, offset]])
        if after is not None:
            ids, _ = lax.optimization_barrier((ids, after))
        return unit_attention(
            queries, ids, kv_head, cache_keys, cache_values, cache_lens, tree_sizes, base, node_count, received
        )

    if owners == 8 and rows_owned == node_count and kv_local == 2:
        r = owner_index
        chip, core = r // 2, r % 2
        cores = [[2 * i, 2 * i + 1] for i in range(4)]
        chips = [[0, 2, 4, 6], [1, 3, 5, 7]]
        ours, theirs = [r ^ 2, r ^ 4, r ^ 6], [r ^ 3, r ^ 5, r ^ 7]
        our_blocks = [chip ^ 1, chip ^ 2, chip ^ 3]
        their_blocks = [4 * (1 - core) + block for block in our_blocks]

        def gather(array, groups):
            return lax.all_gather(array, "req", axis=0, tiled=True, axis_index_groups=groups)

        def send(partials):
            return [exchange(partials[i : i + 1], 2 * (i + 1) + 1) for i in range(3)]

        first = gather(own[0], chips)
        near0 = attend([own[0], exchange(own[0], 1)], [r, r ^ 1], [0, 0], 0)
        first_all = gather(first, cores)
        late, _ = lax.optimization_barrier((own[1], near0))
        second = gather(late, chips)
        second_all = gather(second, cores)
        from_near0 = exchange(near0[1:2], 1)
        tree_partials, tree_logs = attend_tree(near0)
        ours0 = attend(first, ours, our_blocks, 0, after=(tree_logs, from_near0))
        swapped0 = gather(ours0, cores)
        ours1 = attend(second, ours, our_blocks, 1, after=ours0)
        swapped1 = gather(ours1, cores)
        sibling_part = 3 * (1 - core)
        theirs0 = attend(first_all, theirs, their_blocks, 0, swapped0, sibling_part, after=ours1)
        sent0 = send(theirs0)
        theirs1 = attend(second_all, theirs, their_blocks, 1, swapped1, sibling_part, after=theirs0)
        sent1 = send(theirs1)
        near1 = attend(second_all, [r, r ^ 1], [4 * core + chip, 4 * (1 - core) + chip], 1, after=(theirs1, sent0))
        from_near1 = exchange(near1[1:2], 1)
        parts = [
            [(near0, 0), (from_near0, 0)] + [(piece, 0) for piece in sent0],
            [(near1, 0), (from_near1, 0)] + [(piece, 0) for piece in sent1],
        ]
        return merge(parts, tree_partials, tree_logs, alive)

    tree_partials, tree_logs = attend_tree()
    every = [lax.all_gather(q, "req", axis=0, tiled=True) for q in own]
    targets = list(range(requests))
    partials = jnp.stack([attend(every[g], targets, targets, g) for g in range(kv_local)])
    partials = partials.reshape(kv_local, owners, rows_owned, WIDE + LANES)
    partials = lax.all_to_all(partials, "req", split_axis=1, concat_axis=1)
    partials = partials.reshape(kv_local * owners, rows_owned, WIDE + LANES)
    parts = [[(partials, g * owners + j) for j in range(owners)] for g in range(kv_local)]
    return merge(parts, tree_partials, tree_logs, alive)


def solution(mesh):
    placed = (
        P(("req", "head"), None),
        P(None, "req", "head"),
        P(None, "req", "head"),
        P("req", "head"),
        P("req", "head"),
        P(),
        P(),
        P(),
    )
    return jax.shard_map(
        body, mesh=mesh, in_specs=placed, out_specs=P("req", "head"), check_vma=False
    )
```

profile of v0, /device:TPU:0, one launch (start us, length us, event | category | flops | bytes accessed | tf_op | source)
XLA Modules:
  0.0 256.9 jit_solution(13811631427264277903)
XLA Ops:
  6.5 1.4 fusion.2
  7.9 0.1 pad_maximum_fusion
  8.0 20.7 %all_to_all.38 = bf16[32,4,2048]{2,0,1:T(8,128)(2,1)} all-to-all(bf16[32,4,2048]{2,0,1:T(8,128)(2,1)S(1)} %bitcast.40), channel_id=1, replica_groups=mesh['req'=8,'head'=4] {'head'}, dimensions={1} | all-to-all | bytes 1048576 | tf_op jit(solution)/shard_map/all_to_all | solution.py:433
  28.7 0.0 all-gather.7.cloned.1.call-update
  28.8 0.1 collective-permute-start
  28.8 0.8 copy.17
  29.7 3.5 %all-to-all-start.1 = ((bf16[32,4,2048]{2,0,1:T(8,128)(2,1)}), bf16[32,4,2048]{2,0,1:T(8,128)(2,1)S(1)}, u32[]{:S(2)}, u32[]{:S(2)}) async-start(bf16[32,4,2048]{2,0,1:T(8,128)(2,1)} %bitcast.32), calls=%async_computation.1 | async-start | bytes 1048576 | tf_op jit(solution)/shard_map/all_to_all | solution.py:433
  33.2 0.0 all-gather.9.cloned.1.call-start
  33.2 0.6 pad_add_fusion.ids_ref
  33.8 0.0 collective-permute-done.refs_1_
  33.8 0.8 copy-done.13
  34.6 26.0 %shard_map.82.refs_0_ = bf16[2,128,2176]{2,1,0:T(8,128)(2,1)} custom-call(s32[5]{0:T(128)} %pad_add_fusion.ids_ref, s32[8]{0:T(128)} %lens_ref.11, s32[8]{0:T(128)} %sizes_ref.11, s32[1]{0:T(128)} %bitcast.3.base_ref, bf16[128,2048]{1,0:T(8,128)(2,1)} %bitcast.36, bf16[128,2048]{1,0:T(8,128)(2,1)} %copy-done.13, bf16[8,4096,256]{2,1,0:T(8,128)(2,1)} %refs_1_.9, ...), custom_call_target="tpu_custom_call" | custom-call | flops 8589934592 | bytes 6422528 | tf_op jit(solution)/shard_map/pallas_call | solution.py:286
  60.7 0.0 all-to-all-done.1
  60.7 0.8 copy-done.12
  61.5 0.0 all-gather.9.cloned.1.call-update
  61.5 0.0 all-gather.13.cloned.1.call-start
  61.5 1.1 slice.64
  62.6 0.6 collective-permute-start.1
  63.2 0.6 dynamic_slice.7
  63.8 0.6 stack.104.ids_ref
  64.4 0.5 constant_dynamic-slice_fusion.refs_4_
  64.9 1.2 pad_add_fusion.1.first_ref
  66.2 7.3 %shard_map.83 = (f32[2,128,2048]{2,1,0:T(8,128)}, f32[2,128,128]{2,1,0:T(8,128)}) custom-call(s32[2]{0:T(128)} %pad_add_fusion.1.first_ref, bf16[128,2048]{1,0:T(8,128)(2,1)} %bitcast.37, bf16[128,2048]{1,0:T(8,128)(2,1)} %bitcast.39, bf16[128,256]{1,0:T(8,128)(2,1)} %refs_2_.8, bf16[128,256]{1,0:T(8,128)(2,1)} %refs_3_.3, ...), custom_call_target="tpu_custom_call" | custom-call | flops 1000000000 | bytes 10000000 | tf_op jit(solution)/shard_map/pallas_call | solution.py:347
  73.4 0.0 collective-permute-done.1.refs_1_
  73.4 17.8 %shard_map.84 = bf16[3,128,2176]{2,1,0:T(8,128)(2,1)} custom-call(s32[7]{0:T(128)} %stack.104.ids_ref, s32[8]{0:T(128)} %lens_ref.11, s32[8]{0:T(128)} %sizes_ref.11, s32[1]{0:T(128)} %bitcast.3.base_ref, bf16[512,2048]{1,0:T(8,128)(2,1)} %all-gather.7.cloned.1.call-done.refs_0_, bf16[8,4096,256]{2,1,0:T(8,128)(2,1)} %refs_1_.9, bf16[8,4096,256]{2,1,0:T(8,128)(2,1)} %refs_2_.13), custom_call_target="tpu_custom_call" | custom-call | flops 12884901888 | bytes 9633792 | tf_op jit(solution)/shard_map/pallas_call | solution.py:286
  91.2 0.0 all-gather.13.cloned.1.call-update
  91.3 0.0 all-gather.11.cloned.1.call-start
  91.3 0.5 all-gather.11.cloned.1.call-update
  91.8 0.0 all-gather.17.cloned.1.call-start
  91.9 8.7 %all-gather.9.cloned.1.call-done.refs_0_ = bf16[512,2048]{1,0:T(8,128)(2,1)} async-done(((bf16[128,2048]{1,0:T(8,128)(2,1)}), bf16[512,2048]{1,0:T(8,128)(2,1)}) %all-gather.9.cloned.1.call-update) | async-done | bytes 2097168 | tf_op jit(solution)/shard_map/all_gather | solution.py:476
  100.6 17.8 %shard_map.85 = bf16[3,128,2176]{2,1,0:T(8,128)(2,1)} custom-call(s32[7]{0:T(128)} %stack.104.ids_ref, s32[8]{0:T(128)} %lens_ref.11, s32[8]{0:T(128)} %sizes_ref.11, s32[1]{0:T(128)} %bitcast.3.base_ref, bf16[512,2048]{1,0:T(8,128)(2,1)} %all-gather.9.cloned.1.call-done.refs_0_, bf16[8,4096,256]{2,1,0:T(8,128)(2,1)} %refs_1_.9, bf16[8,4096,256]{2,1,0:T(8,128)(2,1)} %refs_2_.13), custom_call_target="tpu_custom_call" | custom-call | flops 12884901888 | bytes 9633792 | tf_op jit(solution)/shard_map/pallas_call | solution.py:286
  118.3 0.0 all-gather.17.cloned.1.call-update
  118.4 13.3 %all-gather.15.cloned.1.call-start = ((), (), s32[]{:S(2)}) async-start(), calls=%async_computation.6 | async-start | bytes 6291456 | tf_op jit(solution)/shard_map/all_gather | solution.py:476
  131.6 0.0 all-gather.15.cloned.1.call-update
  131.7 0.6 stack.109.ids_ref
  132.3 0.7 stack.97.ids_ref
  133.0 24.3 %shard_map.86 = bf16[3,128,2176]{2,1,0:T(8,128)(2,1)} custom-call(s32[7]{0:T(128)} %stack.97.ids_ref, s32[8]{0:T(128)} %lens_ref.11, s32[8]{0:T(128)} %sizes_ref.11, s32[1]{0:T(128)} %bitcast.3.base_ref, bf16[1024,2048]{1,0:T(8,128)(2,1)} %all-gather.11.cloned.1.call-done.refs_0_, bf16[8,4096,256]{2,1,0:T(8,128)(2,1)} %refs_1_.9, ...), custom_call_target="tpu_custom_call" | custom-call | flops 12884901888 | bytes 9633792 | tf_op jit(solution)/shard_map/pallas_call | solution.py:286
  157.3 2.7 %fusion.1 = (bf16[1,128,2176]{2,1,0:T(8,128)(2,1)S(1)}, bf16[1,128,2176]{2,1,0:T(8,128)(2,1)}, bf16[1,128,2176]{2,1,0:T(8,128)(2,1)}) fusion(bf16[3,128,2176]{2,1,0:T(8,128)(2,1)} %shard_map.86), kind=kLoop, calls=%fused_computation.9 | loop fusion | bytes 3342336 | tf_op jit(solution)/shard_map/slice | solution.py:479
  160.0 0.0 collective-permute-start.2
  160.0 0.0 collective-permute-start.3
  160.0 12.4 %collective-permute-start.4 = (bf16[1,128,2176]{2,1,0:T(8,128)(2,1)S(1)}, bf16[1,128,2176]{2,1,0:T(8,128)(2,1)S(1)}, u32[]{:S(2)}, u32[]{:S(2)}) collective-permute-start(bf16[1,128,2176]{2,1,0:T(8,128)(2,1)S(1)} %get-tuple-element.26), channel_id=1, source_target_pairs={{0,28},{4,24},{8,20},{12,16},{16,12},{20,8},{24,4},{28,0},{1,29},{... | collective-permute-start | bytes 1671176 | tf_op jit(solution)/shard_map/ppermute | solution.py:413
  172.5 24.3 %shard_map.87 = bf16[3,128,2176]{2,1,0:T(8,128)(2,1)} custom-call(s32[7]{0:T(128)} %stack.97.ids_ref, s32[8]{0:T(128)} %lens_ref.11, s32[8]{0:T(128)} %sizes_ref.11, s32[1]{0:T(128)} %bitcast.3.base_ref, bf16[1024,2048]{1,0:T(8,128)(2,1)} %all-gather.15.cloned.1.call-done.refs_0_, bf16[8,4096,256]{2,1,0:T(8,128)(2,1)} %refs_1_.9, ...), custom_call_target="tpu_custom_call" | custom-call | flops 12884901888 | bytes 9633792 | tf_op jit(solution)/shard_map/pallas_call | solution.py:286
  196.8 2.6 %fusion = (bf16[1,128,2176]{2,1,0:T(8,128)(2,1)}, bf16[1,128,2176]{2,1,0:T(8,128)(2,1)}, bf16[1,128,2176]{2,1,0:T(8,128)(2,1)}) fusion(bf16[3,128,2176]{2,1,0:T(8,128)(2,1)} %shard_map.87), kind=kLoop, calls=%fused_computation.8 | loop fusion | bytes 3342336 | tf_op jit(solution)/shard_map/slice | solution.py:479
  199.4 0.0 collective-permute-start.6
  199.4 0.0 collective-permute-start.7
  199.4 0.0 collective-permute-done.2.refs_2_
  199.4 0.8 copy-done.5
  200.2 9.2 %collective-permute-start.8 = (bf16[1,128,2176]{2,1,0:T(8,128)(2,1)}, bf16[1,128,2176]{2,1,0:T(8,128)(2,1)}, u32[]{:S(2)}, u32[]{:S(2)}) collective-permute-start(bf16[1,128,2176]{2,1,0:T(8,128)(2,1)} %get-tuple-element.23), channel_id=1, source_target_pairs={{0,28},{4,24},{8,20},{12,16},{16,12},{20,8},{24,4},{28,0},{1,29},{... | collective-permute-start | bytes 1671176 | tf_op jit(solution)/shard_map/ppermute | solution.py:413
  209.3 0.0 collective-permute-done.3.refs_3_
  209.3 0.8 copy-done.7
  210.1 0.0 collective-permute-done.4.refs_4_
  210.1 0.8 copy-done.9
  211.0 25.7 %shard_map.88.refs_5_ = bf16[2,128,2176]{2,1,0:T(8,128)(2,1)} custom-call(s32[5]{0:T(128)} %stack.109.ids_ref, s32[8]{0:T(128)} %lens_ref.11, s32[8]{0:T(128)} %sizes_ref.11, s32[1]{0:T(128)} %bitcast.3.base_ref, bf16[1024,2048]{1,0:T(8,128)(2,1)} %all-gather.15.cloned.1.call-done.refs_0_, bf16[8,4096,256]{2,1,0:T(8,128)(2,1)} %refs_1_.9, ...), custom_call_target="tpu_custom_call" | custom-call | flops 8589934592 | bytes 6422528 | tf_op jit(solution)/shard_map/pallas_call | solution.py:286
  236.7 1.1 slice.68
  237.8 0.1 collective-permute-start.5
  237.8 0.6 compare_convert_fusion
  238.4 0.0 collective-permute-done.7.refs_8_
  238.4 1.3 collective-permute-done.5.refs_6_
  239.8 0.1 broadcast_in_dim.4.alive_ref
  239.9 1.2 copy-done.3
  241.1 1.1 copy-done.6
  242.2 1.1 copy-done.8
  243.2 1.1 copy-done.10
  244.3 5.5 %shard_map.89 = bf16[128,4096]{1,0:T(8,128)(2,1)} custom-call(f32[128,128]{1,0:T(8,128)S(1)} %broadcast_in_dim.4.alive_ref, bf16[2,128,2176]{2,1,0:T(8,128)(2,1)S(1)} %copy-done.2, bf16[1,128,2176]{2,1,0:T(8,128)(2,1)S(1)} %collective-permute-done.1.refs_1_, bf16[1,128,2176]{2,1,0:T(8,128)(2,1)S(1)} %copy-done.6, bf16[1,128,2176]{2,1,0:T(8,128)(2,1)S(1)} %copy-done.8, ...), custom_call_target="tpu_custom_call" | custom-call | tf_op jit(solution)/shard_map/pallas_call | solution.py:393
  (31 shorter events, 0.1 us)
Async XLA Ops:
  6.5 57.9 %copy-start = (s32[8,128]{1,0:T(8,128)S(1)}, s32[8,128]{1,0:T(8,128)}, u32[]{:S(2)}) copy-start(s32[8,128]{1,0:T(8,128)} %param.13) | copy-start | bytes 12292
  6.5 66.9 %all-gather.7.cloned.1.call-start = ((), (), s32[]{:S(2)}) async-start(), calls=%async_computation.2 | async-start | bytes 2621440 | tf_op jit(solution)/shard_map/all_gather | solution.py:476
  28.8 5.1 %collective-permute-start = (bf16[128,2048]{1,0:T(8,128)(2,1)}, bf16[128,2048]{1,0:T(8,128)(2,1)S(1)}, u32[]{:S(2)}, u32[]{:S(2)}) collective-permute-start(bf16[128,2048]{1,0:T(8,128)(2,1)} %bitcast.35), channel_id=1, source_target_pairs={{0,4},{4,0},{8,12},{12,8},{16,20},{20,16},{24,28},{28,24},{1,5},{5... | collective-permute-start | bytes 1572872 | tf_op jit(solution)/shard_map/ppermute | solution.py:413
  29.7 31.0 %all-to-all-start.1 = ((bf16[32,4,2048]{2,0,1:T(8,128)(2,1)}), bf16[32,4,2048]{2,0,1:T(8,128)(2,1)S(1)}, u32[]{:S(2)}, u32[]{:S(2)}) async-start(bf16[32,4,2048]{2,0,1:T(8,128)(2,1)} %bitcast.32), calls=%async_computation.1 | async-start | bytes 1048576 | tf_op jit(solution)/shard_map/all_to_all | solution.py:433
  33.2 67.4 %all-gather.9.cloned.1.call-start = ((), (), s32[]{:S(2)}) async-start(), calls=%async_computation.3 | async-start | bytes 2621440 | tf_op jit(solution)/shard_map/all_gather | solution.py:476
  33.8 0.8 copy-start.13
  34.6 28.6 %copy-start.14 = (s32[8]{0:T(128)S(1)}, s32[8]{0:T(128)}, u32[]{:S(2)}) copy-start(s32[8]{0:T(128)} %sizes_ref.11) | copy-start | bytes 100
  60.7 0.8 copy-start.12
  61.5 71.5 %all-gather.13.cloned.1.call-start = ((), (), s32[]{:S(2)}) async-start(), calls=%async_computation.5 | async-start | bytes 5013504 | tf_op jit(solution)/shard_map/all_gather | solution.py:476
  62.6 10.8 %collective-permute-start.1 = (bf16[1,128,2176]{2,1,0:T(8,128)(2,1)S(1)}, bf16[1,128,2176]{2,1,0:T(8,128)(2,1)S(1)}, u32[]{:S(2)}, u32[]{:S(2)}) collective-permute-start(bf16[1,128,2176]{2,1,0:T(8,128)(2,1)S(1)} %slice.64), channel_id=1, source_target_pairs={{0,4},{4,0},{8,12},{12,8},{16,20},{20,16},{24,28},{28,24},{1,5},{5... | collective-permute-start | bytes 1671176 | tf_op jit(solution)/shard_map/ppermute | solution.py:413
  91.3 41.7 %all-gather.11.cloned.1.call-start = ((), (), s32[]{:S(2)}) async-start(), calls=%async_computation.4 | async-start | bytes 6291456 | tf_op jit(solution)/shard_map/all_gather | solution.py:476
  91.8 80.6 %all-gather.17.cloned.1.call-start = ((), (), s32[]{:S(2)}) async-start(), calls=%async_computation.7 | async-start | bytes 5013504 | tf_op jit(solution)/shard_map/all_gather | solution.py:476
  118.4 54.1 %all-gather.15.cloned.1.call-start = ((), (), s32[]{:S(2)}) async-start(), calls=%async_computation.6 | async-start | bytes 6291456 | tf_op jit(solution)/shard_map/all_gather | solution.py:476
  160.0 39.3 %collective-permute-start.2 = (bf16[1,128,2176]{2,1,0:T(8,128)(2,1)}, bf16[1,128,2176]{2,1,0:T(8,128)(2,1)S(1)}, u32[]{:S(2)}, u32[]{:S(2)}) collective-permute-start(bf16[1,128,2176]{2,1,0:T(8,128)(2,1)} %get-tuple-element.28), channel_id=1, source_target_pairs={{0,12},{4,8},{8,4},{12,0},{16,28},{20,24},{24,20},{28,16},{1,13},{... | collective-permute-start | bytes 1671176 | tf_op jit(solution)/shard_map/ppermute | solution.py:413
  160.0 49.3 %collective-permute-start.3 = (bf16[1,128,2176]{2,1,0:T(8,128)(2,1)}, bf16[1,128,2176]{2,1,0:T(8,128)(2,1)S(1)}, u32[]{:S(2)}, u32[]{:S(2)}) collective-permute-start(bf16[1,128,2176]{2,1,0:T(8,128)(2,1)} %get-tuple-element.27), channel_id=1, source_target_pairs={{0,20},{4,16},{8,28},{12,24},{16,4},{20,0},{24,12},{28,8},{1,21},{... | collective-permute-start | bytes 1671176 | tf_op jit(solution)/shard_map/ppermute | solution.py:413
  160.0 50.1 %collective-permute-start.4 = (bf16[1,128,2176]{2,1,0:T(8,128)(2,1)S(1)}, bf16[1,128,2176]{2,1,0:T(8,128)(2,1)S(1)}, u32[]{:S(2)}, u32[]{:S(2)}) collective-permute-start(bf16[1,128,2176]{2,1,0:T(8,128)(2,1)S(1)} %get-tuple-element.26), channel_id=1, source_target_pairs={{0,28},{4,24},{8,20},{12,16},{16,12},{20,8},{24,4},{28,0},{1,29},{... | collective-permute-start | bytes 1671176 | tf_op jit(solution)/shard_map/ppermute | solution.py:413
  199.4 39.1 %collective-permute-start.6 = (bf16[1,128,2176]{2,1,0:T(8,128)(2,1)}, bf16[1,128,2176]{2,1,0:T(8,128)(2,1)}, u32[]{:S(2)}, u32[]{:S(2)}) collective-permute-start(bf16[1,128,2176]{2,1,0:T(8,128)(2,1)} %get-tuple-element.25), channel_id=1, source_target_pairs={{0,12},{4,8},{8,4},{12,0},{16,28},{20,24},{24,20},{28,16},{1,13},{... | collective-permute-start | bytes 1671176 | tf_op jit(solution)/shard_map/ppermute | solution.py:413
  199.4 39.1 %collective-permute-start.7 = (bf16[1,128,2176]{2,1,0:T(8,128)(2,1)}, bf16[1,128,2176]{2,1,0:T(8,128)(2,1)}, u32[]{:S(2)}, u32[]{:S(2)}) collective-permute-start(bf16[1,128,2176]{2,1,0:T(8,128)(2,1)} %get-tuple-element.24), channel_id=1, source_target_pairs={{0,20},{4,16},{8,28},{12,24},{16,4},{20,0},{24,12},{28,8},{1,21},{... | collective-permute-start | bytes 1671176 | tf_op jit(solution)/shard_map/ppermute | solution.py:413
  199.4 0.8 copy-start.5
  200.2 39.7 %copy-start.2 = (bf16[2,128,2176]{2,1,0:T(8,128)(2,1)S(1)}, bf16[2,128,2176]{2,1,0:T(8,128)(2,1)}, u32[]{:S(2)}) copy-start(bf16[2,128,2176]{2,1,0:T(8,128)(2,1)} %shard_map.82.refs_0_) | copy-start | bytes 3342340
  200.2 39.7 %copy-start.11 = (f32[2,128,128]{2,1,0:T(8,128)S(1)}, f32[2,128,128]{2,1,0:T(8,128)}, u32[]{:S(2)}) copy-start(f32[2,128,128]{2,1,0:T(8,128)} %get-tuple-element.15.refs_11_) | copy-start | bytes 393220
  200.2 38.3 %collective-permute-start.8 = (bf16[1,128,2176]{2,1,0:T(8,128)(2,1)}, bf16[1,128,2176]{2,1,0:T(8,128)(2,1)}, u32[]{:S(2)}, u32[]{:S(2)}) collective-permute-start(bf16[1,128,2176]{2,1,0:T(8,128)(2,1)} %get-tuple-element.23), channel_id=1, source_target_pairs={{0,28},{4,24},{8,20},{12,16},{16,12},{20,8},{24,4},{28,0},{1,29},{... | collective-permute-start | bytes 1671176 | tf_op jit(solution)/shard_map/ppermute | solution.py:413
  209.3 0.8 copy-start.7
  210.1 0.8 copy-start.9
  211.0 28.9 %copy-start.4 = (f32[2,128,2048]{2,1,0:T(8,128)S(1)}, f32[2,128,2048]{2,1,0:T(8,128)}, u32[]{:S(2)}) copy-start(f32[2,128,2048]{2,1,0:T(8,128)} %get-tuple-element.22.refs_10_) | copy-start | bytes 6291460
  237.8 2.0 collective-permute-start.5
  239.9 1.2 copy-start.3
  241.1 1.1 copy-start.6
  242.2 1.1 copy-start.8
  243.2 1.1 copy-start.10
  244.3 5.5 %copy-start.1 = (s32[8,128]{1,0:T(8,128)S(1)}, s32[8,128]{1,0:T(8,128)}, u32[]{:S(2)}) copy-start(s32[8,128]{1,0:T(8,128)} %param.13) | copy-start | bytes 12292
Sparse Core Ops, SparseCore 0:
  28.9 34.4 all-gather.6
  65.2 35.2 all-gather.8
  102.1 12.4 all-gather.12
  116.1 14.8 all-gather.10
  132.3 13.6 all-gather.16
  147.4 14.7 all-gather.14
where the time goes:
time: 262 us; the launch traced here: 257 us
  Pallas kernels  149 us (57%)
  starting transfers between devices  39.2 us (15%)
  local copies, waits for them, and re-layouts  21.3 us (8%)
  blocking collectives  20.7 us (8%)
  between operations  13.9 us (5%)
  waiting for transfers between devices  10.7 us (4%)
    pallas_call x6, Pallas kernels, unit_attention(): pl.pallas_call(functools.partial(unit_kernel, len(queries), merging, chun...  136 us
    ppermute x9, starting transfers between devices, exchange(): lax.ppermute(array, 'req', [(r, r ^ distance) for r in range(owners)])  22.3 us
    all_to_all x1, blocking collectives, body(): lax.all_to_all(mine, 'head', split_axis=1, concat_axis=0, tiled=True)  20.7 us
    all_gather x6, starting transfers between devices, gather(): lax.all_gather(array, 'req', axis=0, tiled=True, axis_index_groups=groups)  13.5 us
    all_gather x6, waiting for transfers between devices, gather(): lax.all_gather(array, 'req', axis=0, tiled=True, axis_index_groups=groups)  8.69 us
    unnamed x30, local copies, waits for them, and re-layouts  8.42 us
    pallas_call x1, Pallas kernels, tree_attention(): pl.pallas_call(tree_kernel, in_specs=[pl.BlockSpec(memory_space=pltpu.SME...  7.26 us
    pallas_call x1, Pallas kernels, merge(): pl.pallas_call(functools.partial(merge_kernel, [len(of_head) for of_head...  5.52 us
  transfers between devices with their start and end apart: 16, of which 2 were waited for; matrix products, arithmetic and copies ran while one was open for 5% of the time, Pallas kernels for 56%

commit v1 on v0

--- a/solution.py
+++ b/solution.py
@@ -287,7 +287,7 @@
         functools.partial(unit_kernel, len(queries), merging, chunk),
         grid_spec=grid_spec,
         out_shape=jax.ShapeDtypeStruct((units, node_count, width), wire),
-        compiler_params=pltpu.CompilerParams(vmem_limit_bytes=60 * 1024 * 1024),
+        compiler_params=pltpu.CompilerParams(vmem_limit_bytes=56 * 1024 * 1024),
         cost_estimate=pl.CostEstimate(
             flops=4 * units * node_count * GROUP * block * HD,
             bytes_accessed=units * (4 * block * HD + 4 * node_count * width),
@@ -316,7 +316,7 @@
         keys = k_ref[:, g * HD : (g + 1) * HD]
         values = v_ref[:, g * HD : (g + 1) * HD]
 
-        @pl.loop(0, jnp.clip((first_ref[1] - first_ref[0] + tile - 1) // tile, 0, rows_owned // tile))
+        @pl.loop(0, rows_owned // tile)
         def _(t):
             start = pl.multiple_of(t * tile, tile)
             first = pl.multiple_of(first_ref[0] + start, tile)
@@ -353,7 +353,7 @@
             jax.ShapeDtypeStruct((kv_local, rows, LANES), jnp.float32),
         ],
         scratch_shapes=[pltpu.VMEM((node_count, node_count), jnp.float32)],
-        compiler_params=pltpu.CompilerParams(vmem_limit_bytes=60 * 1024 * 1024),
+        compiler_params=pltpu.CompilerParams(vmem_limit_bytes=56 * 1024 * 1024),
         cost_estimate=pl.CostEstimate(flops=10**9, bytes_accessed=10**7, transcendentals=10**6),
     )(first, *queries, keys, values, parents)
 
@@ -404,7 +404,7 @@
         ],
         out_specs=pl.BlockSpec((tile, kv_local * WIDE), lambda i: (i, 0)),
         out_shape=jax.ShapeDtypeStruct((rows, kv_local * WIDE), jnp.bfloat16),
-        compiler_params=pltpu.CompilerParams(vmem_limit_bytes=40 * 1024 * 1024),
+        compiler_params=pltpu.CompilerParams(vmem_limit_bytes=48 * 1024 * 1024),
     )(alive, *[array for array, _ in flat], tree_partials, tree_logs)
 
 
@@ -446,7 +446,7 @@
     own_parents = lax.dynamic_slice_in_dim(parents, request, 1, 0)
 
     def attend_tree(after=None):
-        first = jnp.stack([first_node, size])
+        first = first_node[None]
         if after is not None:
             first, _ = lax.optimization_barrier((first, after))
         return tree_attention(own, own_keys, own_values, own_parents, first)
@@ -465,37 +465,32 @@
 
     if owners == 8 and rows_owned == node_count and kv_local == 2:
         r = owner_index
-        chip, core = r // 2, r % 2
+        core = r % 2
         cores = [[2 * i, 2 * i + 1] for i in range(4)]
-        chips = [[0, 2, 4, 6], [1, 3, 5, 7]]
         ours, theirs = [r ^ 2, r ^ 4, r ^ 6], [r ^ 3, r ^ 5, r ^ 7]
-        our_blocks = [chip ^ 1, chip ^ 2, chip ^ 3]
-        their_blocks = [4 * (1 - core) + block for block in our_blocks]
-
-        def gather(array, groups):
-            return lax.all_gather(array, "req", axis=0, tiled=True, axis_index_groups=groups)
+
+        def swap(partials):
+            return lax.all_gather(partials, "req", axis=0, tiled=True, axis_index_groups=cores)
 
         def send(partials):
             return [exchange(partials[i : i + 1], 2 * (i + 1) + 1) for i in range(3)]
 
-        first = gather(own[0], chips)
+        first = lax.all_gather(own[0], "req", axis=0, tiled=True)
         near0 = attend([own[0], exchange(own[0], 1)], [r, r ^ 1], [0, 0], 0)
-        first_all = gather(first, cores)
         late, _ = lax.optimization_barrier((own[1], near0))
-        second = gather(late, chips)
-        second_all = gather(second, cores)
+        second = lax.all_gather(late, "req", axis=0, tiled=True)
         from_near0 = exchange(near0[1:2], 1)
         tree_partials, tree_logs = attend_tree(near0)
-        ours0 = attend(first, ours, our_blocks, 0, after=(tree_logs, from_near0))
-        swapped0 = gather(ours0, cores)
-        ours1 = attend(second, ours, our_blocks, 1, after=ours0)
-        swapped1 = gather(ours1, cores)
+        ours0 = attend(first, ours, ours, 0, after=(tree_logs, from_near0))
+        swapped0 = swap(ours0)
+        ours1 = attend(second, ours, ours, 1, after=ours0)
+        swapped1 = swap(ours1)
         sibling_part = 3 * (1 - core)
-        theirs0 = attend(first_all, theirs, their_blocks, 0, swapped0, sibling_part, after=ours1)
+        theirs0 = attend(first, theirs, theirs, 0, swapped0, sibling_part, after=ours1)
         sent0 = send(theirs0)
-        theirs1 = attend(second_all, theirs, their_blocks, 1, swapped1, sibling_part, after=theirs0)
+        theirs1 = attend(second, theirs, theirs, 1, swapped1, sibling_part, after=theirs0)
         sent1 = send(theirs1)
-        near1 = attend(second_all, [r, r ^ 1], [4 * core + chip, 4 * (1 - core) + chip], 1, after=(theirs1, sent0))
+        near1 = attend(second, [r, r ^ 1], [r, r ^ 1], 1, after=(theirs1, sent0))
         from_near1 = exchange(near1[1:2], 1)
         parts = [
             [(near0, 0), (from_near0, 0)] + [(piece, 0) for piece in sent0],

time: 262 us -> 245 us (0.935)
  starting transfers between devices: 39.2 us -> 14.1 us
  waiting for transfers between devices: 10.7 us -> 26 us
  local copies, waits for them, and re-layouts: 21.3 us -> 13.9 us
    all_gather x6 -> x4, starting transfers between devices: 13.5 us -> 0.51 us  [the longest x2 0.47 us: swap(): lax.all_gather(partials, 'req', axis=0, tiled=True, axis_index_groups=cores)]
    ppermute x9, starting transfers between devices: 22.3 us -> 10.2 us  [exchange(): lax.ppermute(array, 'req', [(r, r ^ distance) for r in range(owners)])]
    all_gather x6 -> x4, waiting for transfers between devices: 8.69 us -> 17.6 us  [the longest x1 11.8 us: body(): second = lax.all_gather(late, 'req', axis=0, tiled=True)]
    unnamed x30 -> x14, local copies, waits for them, and re-layouts: 8.42 us -> 1.61 us
    ppermute x9, waiting for transfers between devices: 1.35 us -> 6.76 us  [exchange(): lax.ppermute(array, 'req', [(r, r ^ distance) for r in range(owners)])]
  transfers between devices with their start and end apart: 16 -> 14, of which waited for: 2 -> 4; matrix products, arithmetic and copies ran while one was open for 5% -> 5% of each run, Pallas kernels for 56% -> 60%
where the time goes in v1:
time: 245 us; the launch traced here: 240 us
  Pallas kernels  150 us (61%)
  waiting for transfers between devices  26 us (11%)
  blocking collectives  20.7 us (8%)
  starting transfers between devices  14.1 us (6%)
  local copies, waits for them, and re-layouts  13.9 us (6%)
  between operations  13.8 us (6%)
    pallas_call x6, Pallas kernels, unit_attention(): pl.pallas_call(functools.partial(unit_kernel, len(queries), merging, chun...  138 us
    all_to_all x1, blocking collectives, body(): lax.all_to_all(mine, 'head', split_axis=1, concat_axis=0, tiled=True)  20.7 us
    all_gather x1, waiting for transfers between devices, body(): second = lax.all_gather(late, 'req', axis=0, tiled=True)  11.8 us
    ppermute x9, starting transfers between devices, exchange(): lax.ppermute(array, 'req', [(r, r ^ distance) for r in range(owners)])  10.2 us
    pallas_call x1, Pallas kernels, tree_attention(): pl.pallas_call(tree_kernel, in_specs=[pl.BlockSpec(memory_space=pltpu.SME...  6.96 us
    ppermute x9, waiting for transfers between devices, exchange(): lax.ppermute(array, 'req', [(r, r ^ distance) for r in range(owners)])  6.76 us
    all_gather x1, waiting for transfers between devices, body(): first = lax.all_gather(own[0], 'req', axis=0, tiled=True)  5.8 us
    pallas_call x1, Pallas kernels, merge(): pl.pallas_call(functools.partial(merge_kernel, [len(of_head) for of_head...  5.66 us
  transfers between devices with their start and end apart: 14, of which 4 were waited for; matrix products, arithmetic and copies ran while one was open for 5% of the time, Pallas kernels for 60%

profile of v1, /device:TPU:0, one launch (start us, length us, event | category | flops | bytes accessed | tf_op | source)
XLA Modules:
  0.0 240.2 jit_solution(7423029196103887797)
XLA Ops:
  6.5 0.0 copy-start
  6.5 0.0 all-gather.5.cloned.1.call-start
  6.5 1.4 fusion.2
  7.9 0.1 pad_maximum_fusion
  8.0 20.7 %all_to_all.38 = bf16[32,4,2048]{2,0,1:T(8,128)(2,1)} all-to-all(bf16[32,4,2048]{2,0,1:T(8,128)(2,1)S(1)} %bitcast.32), channel_id=1, replica_groups=mesh['req'=8,'head'=4] {'head'}, dimensions={1} | all-to-all | bytes 1048576 | tf_op jit(solution)/shard_map/all_to_all | solution.py:433
  28.7 0.0 all-gather.5.cloned.1.call-update
  28.8 0.1 collective-permute-start
  28.8 0.9 copy.17
  29.7 3.5 %all-to-all-start.1 = ((bf16[32,4,2048]{2,0,1:T(8,128)(2,1)}), bf16[32,4,2048]{2,0,1:T(8,128)(2,1)S(1)}, u32[]{:S(2)}, u32[]{:S(2)}) async-start(bf16[32,4,2048]{2,0,1:T(8,128)(2,1)} %bitcast.24), calls=%async_computation.1 | async-start | bytes 1048576 | tf_op jit(solution)/shard_map/all_to_all | solution.py:433
  33.2 0.0 all-gather.7.cloned.1.call-start
  33.3 0.6 pad_add_fusion.ids_ref
  33.9 0.0 collective-permute-done.refs_1_
  33.9 0.8 copy-done.5
  34.7 12.4 %shard_map.82.refs_0_ = bf16[2,128,2176]{2,1,0:T(8,128)(2,1)} custom-call(s32[5]{0:T(128)} %pad_add_fusion.ids_ref, s32[8]{0:T(128)} %lens_ref.11, s32[8]{0:T(128)} %sizes_ref.11, s32[1]{0:T(128)} %bitcast.3.base_ref, bf16[128,2048]{1,0:T(8,128)(2,1)} %bitcast.28, bf16[128,2048]{1,0:T(8,128)(2,1)} %copy-done.5, bf16[8,4096,256]{2,1,0:T(8,128)(2,1)} %refs_1_.9, ...), custom_call_target="tpu_custom_call" | custom-call | flops 8589934592 | bytes 6422528 | tf_op jit(solution)/shard_map/pallas_call | solution.py:286
  47.0 1.6 all-to-all-done.1
  48.6 0.8 copy-done.4
  49.4 0.0 all-gather.7.cloned.1.call-update
  49.4 0.2 all-gather.9.cloned.1.call-start
  49.6 1.2 slice.64
  50.8 0.1 collective-permute-start.1
  50.9 0.6 stack.37.ids_ref
  51.5 0.0 copy-done
  51.5 0.5 constant_dynamic-slice_fusion.refs_4_
  52.1 7.0 %shard_map.83 = (f32[2,128,2048]{2,1,0:T(8,128)}, f32[2,128,128]{2,1,0:T(8,128)}) custom-call(s32[1]{0:T(128)} %bitcast.14.first_ref, bf16[128,2048]{1,0:T(8,128)(2,1)} %bitcast.29, bf16[128,2048]{1,0:T(8,128)(2,1)} %bitcast.31, bf16[128,256]{1,0:T(8,128)(2,1)} %refs_2_.8, bf16[128,256]{1,0:T(8,128)(2,1)} %refs_3_.3, s32[1,128]{1,0:T(1,128)} %constant_dynamic-slice_fusion.refs_4_), custom_call_target="tpu_custom_call" | custom-call | flops 1000000000 | bytes 10000000 | tf_op jit(solution)/shard_map/pallas_call | solution.py:347
  59.0 0.0 collective-permute-done.1.refs_1_
  59.0 5.8 %all-gather.5.cloned.1.call-done.refs_0_ = bf16[1024,2048]{1,0:T(8,128)(2,1)} async-done(((bf16[128,2048]{1,0:T(8,128)(2,1)}), bf16[1024,2048]{1,0:T(8,128)(2,1)}) %all-gather.5.cloned.1.call-update) | async-done | bytes 4194320 | tf_op jit(solution)/shard_map/all_gather | solution.py:478
  64.8 26.6 %shard_map.84 = bf16[3,128,2176]{2,1,0:T(8,128)(2,1)} custom-call(s32[7]{0:T(128)} %stack.37.ids_ref, s32[8]{0:T(128)} %lens_ref.11, s32[8]{0:T(128)} %sizes_ref.11, s32[1]{0:T(128)} %bitcast.3.base_ref, bf16[1024,2048]{1,0:T(8,128)(2,1)} %all-gather.5.cloned.1.call-done.refs_0_, bf16[8,4096,256]{2,1,0:T(8,128)(2,1)} %refs_1_.9, bf16[8,4096,256]{2,1,0:T(8,128)(2,1)} %refs_2_.13), custom_call_target="tpu_custom_call" | custom-call | flops 12884901888 | bytes 9633792 | tf_op jit(solution)/shard_map/pallas_call | solution.py:286
  91.4 0.0 all-gather.9.cloned.1.call-update
  91.4 0.3 all-gather.11.cloned.1.call-start
  91.7 11.8 %all-gather.7.cloned.1.call-done.refs_0_ = bf16[1024,2048]{1,0:T(8,128)(2,1)} async-done(((bf16[128,2048]{1,0:T(8,128)(2,1)}), bf16[1024,2048]{1,0:T(8,128)(2,1)}) %all-gather.7.cloned.1.call-update) | async-done | bytes 4194320 | tf_op jit(solution)/shard_map/all_gather | solution.py:481
  103.5 26.6 %shard_map.85 = bf16[3,128,2176]{2,1,0:T(8,128)(2,1)} custom-call(s32[7]{0:T(128)} %stack.37.ids_ref, s32[8]{0:T(128)} %lens_ref.11, s32[8]{0:T(128)} %sizes_ref.11, s32[1]{0:T(128)} %bitcast.3.base_ref, bf16[1024,2048]{1,0:T(8,128)(2,1)} %all-gather.7.cloned.1.call-done.refs_0_, bf16[8,4096,256]{2,1,0:T(8,128)(2,1)} %refs_1_.9, bf16[8,4096,256]{2,1,0:T(8,128)(2,1)} %refs_2_.13), custom_call_target="tpu_custom_call" | custom-call | flops 12884901888 | bytes 9633792 | tf_op jit(solution)/shard_map/pallas_call | solution.py:286
  130.0 0.0 all-gather.11.cloned.1.call-update
  130.1 0.6 stack.76.ids_ref
  130.7 0.6 stack.33.ids_ref
  131.3 30.0 %shard_map.86 = bf16[3,128,2176]{2,1,0:T(8,128)(2,1)} custom-call(s32[7]{0:T(128)} %stack.33.ids_ref, s32[8]{0:T(128)} %lens_ref.11, s32[8]{0:T(128)} %sizes_ref.11, s32[1]{0:T(128)} %bitcast.3.base_ref, bf16[1024,2048]{1,0:T(8,128)(2,1)} %all-gather.5.cloned.1.call-done.refs_0_, bf16[8,4096,256]{2,1,0:T(8,128)(2,1)} %refs_1_.9, ...), custom_call_target="tpu_custom_call" | custom-call | flops 12884901888 | bytes 9633792 | tf_op jit(solution)/shard_map/pallas_call | solution.py:286
  161.3 2.3 fusion.1
  163.6 0.0 collective-permute-start.2
  163.6 0.0 collective-permute-start.3
  163.6 9.9 %collective-permute-start.4 = (bf16[1,128,2176]{2,1,0:T(8,128)(2,1)S(1)}, bf16[1,128,2176]{2,1,0:T(8,128)(2,1)S(1)}, u32[]{:S(2)}, u32[]{:S(2)}) collective-permute-start(bf16[1,128,2176]{2,1,0:T(8,128)(2,1)S(1)} %get-tuple-element.26), channel_id=1, source_target_pairs={{0,28},{4,24},{8,20},{12,16},{16,12},{20,8},{24,4},{28,0},{1,29},{... | collective-permute-start | bytes 1671176 | tf_op jit(solution)/shard_map/ppermute | solution.py:413
  173.5 30.2 %shard_map.87 = bf16[3,128,2176]{2,1,0:T(8,128)(2,1)} custom-call(s32[7]{0:T(128)} %stack.33.ids_ref, s32[8]{0:T(128)} %lens_ref.11, s32[8]{0:T(128)} %sizes_ref.11, s32[1]{0:T(128)} %bitcast.3.base_ref, bf16[1024,2048]{1,0:T(8,128)(2,1)} %all-gather.7.cloned.1.call-done.refs_0_, bf16[8,4096,256]{2,1,0:T(8,128)(2,1)} %refs_1_.9, ...), custom_call_target="tpu_custom_call" | custom-call | flops 12884901888 | bytes 9633792 | tf_op jit(solution)/shard_map/pallas_call | solution.py:286
  203.7 2.3 fusion
  206.0 0.0 collective-permute-start.6
  206.0 0.0 collective-permute-start.7
  206.0 0.0 collective-permute-done.2.refs_2_
  206.0 0.0 copy-start.6
  206.1 0.0 copy-start.3
  206.1 0.1 collective-permute-start.8
  206.2 0.0 collective-permute-done.3.refs_3_
  206.2 0.0 collective-permute-done.4.refs_4_
  206.2 12.0 %shard_map.88.refs_5_ = bf16[2,128,2176]{2,1,0:T(8,128)(2,1)} custom-call(s32[5]{0:T(128)} %stack.76.ids_ref, s32[8]{0:T(128)} %lens_ref.11, s32[8]{0:T(128)} %sizes_ref.11, s32[1]{0:T(128)} %bitcast.3.base_ref, bf16[1024,2048]{1,0:T(8,128)(2,1)} %all-gather.7.cloned.1.call-done.refs_0_, bf16[8,4096,256]{2,1,0:T(8,128)(2,1)} %refs_1_.9, ...), custom_call_target="tpu_custom_call" | custom-call | flops 8589934592 | bytes 6422528 | tf_op jit(solution)/shard_map/pallas_call | solution.py:286
  218.2 1.2 slice.68
  219.4 0.1 collective-permute-start.5
  219.5 0.0 copy-done.6
  219.5 0.6 dynamic_slice.7
  220.1 0.6 compare_convert_fusion
  220.7 0.0 collective-permute-done.6.refs_7_
  220.7 6.7 %collective-permute-done.7.refs_8_ = bf16[1,128,2176]{2,1,0:T(8,128)(2,1)S(1)} collective-permute-done((bf16[1,128,2176]{2,1,0:T(8,128)(2,1)S(1)}, bf16[1,128,2176]{2,1,0:T(8,128)(2,1)S(1)}, u32[]{:S(2)}, u32[]{:S(2)}) %collective-permute-start.7) | collective-permute-done | bytes 557088 | tf_op jit(solution)/shard_map/ppermute | solution.py:413
  227.5 0.0 collective-permute-done.8.refs_9_
  227.5 0.0 collective-permute-done.5.refs_6_
  227.5 0.1 broadcast_in_dim.12.alive_ref
  227.6 0.0 copy-done.3
  227.6 0.0 copy-done.2
  227.6 0.0 copy-start.1
  227.6 5.7 %shard_map.89 = bf16[128,4096]{1,0:T(8,128)(2,1)} custom-call(f32[128,128]{1,0:T(8,128)S(1)} %broadcast_in_dim.12.alive_ref, bf16[2,128,2176]{2,1,0:T(8,128)(2,1)S(1)} %copy-done.2, bf16[1,128,2176]{2,1,0:T(8,128)(2,1)S(1)} %collective-permute-done.1.refs_1_, bf16[1,128,2176]{2,1,0:T(8,128)(2,1)S(1)} %collective-permute-done.2.refs_2_, ...), custom_call_target="tpu_custom_call" | custom-call | tf_op jit(solution)/shard_map/pallas_call | solution.py:393
  (8 shorter events, 0.0 us)
Async XLA Ops:
  6.5 45.0 %copy-start = (s32[8,128]{1,0:T(8,128)S(1)}, s32[8,128]{1,0:T(8,128)}, u32[]{:S(2)}) copy-start(s32[8,128]{1,0:T(8,128)} %param.13) | copy-start | bytes 12292
  6.5 58.3 %all-gather.5.cloned.1.call-start = ((), (), s32[]{:S(2)}) async-start(), calls=%async_computation.2 | async-start | bytes 4718592 | tf_op jit(solution)/shard_map/all_gather | solution.py:478
  28.8 5.1 %collective-permute-start = (bf16[128,2048]{1,0:T(8,128)(2,1)}, bf16[128,2048]{1,0:T(8,128)(2,1)S(1)}, u32[]{:S(2)}, u32[]{:S(2)}) collective-permute-start(bf16[128,2048]{1,0:T(8,128)(2,1)} %bitcast.27), channel_id=1, source_target_pairs={{0,4},{4,0},{8,12},{12,8},{16,20},{20,16},{24,28},{28,24},{1,5},{5... | collective-permute-start | bytes 1572872 | tf_op jit(solution)/shard_map/ppermute | solution.py:413
  29.7 18.9 %all-to-all-start.1 = ((bf16[32,4,2048]{2,0,1:T(8,128)(2,1)}), bf16[32,4,2048]{2,0,1:T(8,128)(2,1)S(1)}, u32[]{:S(2)}, u32[]{:S(2)}) async-start(bf16[32,4,2048]{2,0,1:T(8,128)(2,1)} %bitcast.24), calls=%async_computation.1 | async-start | bytes 1048576 | tf_op jit(solution)/shard_map/all_to_all | solution.py:433
  33.2 70.3 %all-gather.7.cloned.1.call-start = ((), (), s32[]{:S(2)}) async-start(), calls=%async_computation.3 | async-start | bytes 4718592 | tf_op jit(solution)/shard_map/all_gather | solution.py:481
  33.9 0.8 copy-start.5
  48.6 0.8 copy-start.4
  49.4 81.9 %all-gather.9.cloned.1.call-start = ((), (), s32[]{:S(2)}) async-start(), calls=%async_computation.4 | async-start | bytes 5013504 | tf_op jit(solution)/shard_map/all_gather | solution.py:473
  50.8 8.2 %collective-permute-start.1 = (bf16[1,128,2176]{2,1,0:T(8,128)(2,1)S(1)}, bf16[1,128,2176]{2,1,0:T(8,128)(2,1)S(1)}, u32[]{:S(2)}, u32[]{:S(2)}) collective-permute-start(bf16[1,128,2176]{2,1,0:T(8,128)(2,1)S(1)} %slice.64), channel_id=1, source_target_pairs={{0,4},{4,0},{8,12},{12,8},{16,20},{20,16},{24,28},{28,24},{1,5},{5... | collective-permute-start | bytes 1671176 | tf_op jit(solution)/shard_map/ppermute | solution.py:413
  91.4 82.1 %all-gather.11.cloned.1.call-start = ((), (), s32[]{:S(2)}) async-start(), calls=%async_computation.5 | async-start | bytes 5013504 | tf_op jit(solution)/shard_map/all_gather | solution.py:473
  163.6 42.4 %collective-permute-start.2 = (bf16[1,128,2176]{2,1,0:T(8,128)(2,1)}, bf16[1,128,2176]{2,1,0:T(8,128)(2,1)S(1)}, u32[]{:S(2)}, u32[]{:S(2)}) collective-permute-start(bf16[1,128,2176]{2,1,0:T(8,128)(2,1)} %get-tuple-element.28), channel_id=1, source_target_pairs={{0,12},{4,8},{8,4},{12,0},{16,28},{20,24},{24,20},{28,16},{1,13},{... | collective-permute-start | bytes 1671176 | tf_op jit(solution)/shard_map/ppermute | solution.py:413
  163.6 42.5 %collective-permute-start.3 = (bf16[1,128,2176]{2,1,0:T(8,128)(2,1)S(1)}, bf16[1,128,2176]{2,1,0:T(8,128)(2,1)S(1)}, u32[]{:S(2)}, u32[]{:S(2)}) collective-permute-start(bf16[1,128,2176]{2,1,0:T(8,128)(2,1)S(1)} %get-tuple-element.27), channel_id=1, source_target_pairs={{0,20},{4,16},{8,28},{12,24},{16,4},{20,0},{24,12},{28,8},{1,21},{... | collective-permute-start | bytes 1671176 | tf_op jit(solution)/shard_map/ppermute | solution.py:413
  163.6 42.5 %collective-permute-start.4 = (bf16[1,128,2176]{2,1,0:T(8,128)(2,1)S(1)}, bf16[1,128,2176]{2,1,0:T(8,128)(2,1)S(1)}, u32[]{:S(2)}, u32[]{:S(2)}) collective-permute-start(bf16[1,128,2176]{2,1,0:T(8,128)(2,1)S(1)} %get-tuple-element.26), channel_id=1, source_target_pairs={{0,28},{4,24},{8,20},{12,16},{16,12},{20,8},{24,4},{28,0},{1,29},{... | collective-permute-start | bytes 1671176 | tf_op jit(solution)/shard_map/ppermute | solution.py:413
  206.0 14.7 %collective-permute-start.6 = (bf16[1,128,2176]{2,1,0:T(8,128)(2,1)}, bf16[1,128,2176]{2,1,0:T(8,128)(2,1)S(1)}, u32[]{:S(2)}, u32[]{:S(2)}) collective-permute-start(bf16[1,128,2176]{2,1,0:T(8,128)(2,1)} %get-tuple-element.25), channel_id=1, source_target_pairs={{0,12},{4,8},{8,4},{12,0},{16,28},{20,24},{24,20},{28,16},{1,13},{... | collective-permute-start | bytes 1671176 | tf_op jit(solution)/shard_map/ppermute | solution.py:413
  206.0 21.4 %collective-permute-start.7 = (bf16[1,128,2176]{2,1,0:T(8,128)(2,1)S(1)}, bf16[1,128,2176]{2,1,0:T(8,128)(2,1)S(1)}, u32[]{:S(2)}, u32[]{:S(2)}) collective-permute-start(bf16[1,128,2176]{2,1,0:T(8,128)(2,1)S(1)} %get-tuple-element.24), channel_id=1, source_target_pairs={{0,20},{4,16},{8,28},{12,24},{16,4},{20,0},{24,12},{28,8},{1,21},{... | collective-permute-start | bytes 1671176 | tf_op jit(solution)/shard_map/ppermute | solution.py:413
  206.0 13.4 %copy-start.6 = (s32[8]{0:T(128)S(1)}, s32[8]{0:T(128)}, u32[]{:S(2)}) copy-start(s32[8]{0:T(128)} %sizes_ref.11) | copy-start | bytes 100
  206.1 21.5 %copy-start.3 = (f32[2,128,128]{2,1,0:T(8,128)S(1)}, f32[2,128,128]{2,1,0:T(8,128)}, u32[]{:S(2)}) copy-start(f32[2,128,128]{2,1,0:T(8,128)} %get-tuple-element.15.refs_11_) | copy-start | bytes 393220
  206.1 21.4 %collective-permute-start.8 = (bf16[1,128,2176]{2,1,0:T(8,128)(2,1)S(1)}, bf16[1,128,2176]{2,1,0:T(8,128)(2,1)S(1)}, u32[]{:S(2)}, u32[]{:S(2)}) collective-permute-start(bf16[1,128,2176]{2,1,0:T(8,128)(2,1)S(1)} %get-tuple-element.23), channel_id=1, source_target_pairs={{0,28},{4,24},{8,20},{12,16},{16,12},{20,8},{24,4},{28,0},{1,29},{... | collective-permute-start | bytes 1671176 | tf_op jit(solution)/shard_map/ppermute | solution.py:413
  218.2 9.4 %copy-start.2 = (bf16[2,128,2176]{2,1,0:T(8,128)(2,1)S(1)}, bf16[2,128,2176]{2,1,0:T(8,128)(2,1)}, u32[]{:S(2)}) copy-start(bf16[2,128,2176]{2,1,0:T(8,128)(2,1)} %shard_map.82.refs_0_) | copy-start | bytes 3342340
  219.4 8.1 %collective-permute-start.5 = (bf16[1,128,2176]{2,1,0:T(8,128)(2,1)S(1)}, bf16[1,128,2176]{2,1,0:T(8,128)(2,1)S(1)}, u32[]{:S(2)}, u32[]{:S(2)}) collective-permute-start(bf16[1,128,2176]{2,1,0:T(8,128)(2,1)S(1)} %slice.68), channel_id=1, source_target_pairs={{0,4},{4,0},{8,12},{12,8},{16,20},{20,16},{24,28},{28,24},{1,5},{5... | collective-permute-start | bytes 1671176 | tf_op jit(solution)/shard_map/ppermute | solution.py:413
  227.6 5.7 %copy-start.1 = (s32[8,128]{1,0:T(8,128)S(1)}, s32[8,128]{1,0:T(8,128)}, u32[]{:S(2)}) copy-start(s32[8,128]{1,0:T(8,128)} %param.13) | copy-start | bytes 12292
Sparse Core Ops, SparseCore 0:
  28.9 35.8 all-gather.4
  66.7 36.7 all-gather.6
  105.0 12.4 all-gather.8
  130.2 21.0 all-gather.10
